TPU v7x, 128 devices: a whole 4x4x4 slice. The times are simulated.
128 devices in a mesh: section: 8 (over y, x_lo), fsdp: 16 (over z, x_hi, core).
Axes of the slice: x: 4 (x_hi: 2, x_lo: 2; x = x_hi * 2 + x_lo), y: 4, z: 4, core: 2. Of those that a mesh axis runs over, the one named last changes fastest.
Arguments:
- inputs: bfloat16 [8, 2, 2048, 8192], P('section', None, 'fsdp'), may hold values from -6 to 6
- queries: bfloat16 [8, 2, 2048, 8192], P('section', None, 'fsdp'), may hold values from -14 to 14, as said below
- top_cotangent: bfloat16 [2, 2048, 8192], P(None, 'fsdp'), may hold values from -6 to 6
- key_weight: bfloat16 [8, 8192, 512], P('section', 'fsdp'), may hold values from -0.0625 to 0.0625
- value_weight: bfloat16 [8, 8192, 512], P('section', 'fsdp'), may hold values from -0.0625 to 0.0625
- order: int32 [2], replicated, may hold values from 0 to 1, each once
- doc_lengths: int32 [2, 16, 4], P(None, 'fsdp'), may hold values from 1 to 64, 128 in all within a row
Outputs:
- grads: bfloat16 [8, 2, 2048, 8192], P('section', None, 'fsdp')
Inputs may be any that keep to these rules, and one draw needn't show every extreme that they name: `queries`: query entries are of order one, or rows scaled by up to 8. `doc_lengths`: each row sums to 128; the largest length is 64.
All inputs are finite; a program needn't handle non-finite values.
Results may differ from a plain program's by a relative error of at most 0.035.
Values may be sent and summed in bfloat16 or wider, within the bound.
A program may use at most 128 MiB of HBM per device.

v0:
```python
import jax
import jax.numpy as jnp
from jax import lax
from jax.sharding import PartitionSpec as P

HEADS = 64
KV_HEADS = 4
HEAD_DIM = 128


def passed_along(value, axis, steps):
    count = lax.axis_size(axis)
    initial, last = (max(0, -steps), min(count, count - steps))
    return lax.ppermute(value, axis, [(source, source + steps) for source in range(initial, last)])


def segment_ids(lengths, rows):
    ends = jnp.cumsum(lengths)
    pos = jnp.arange(rows, dtype=jnp.int32)
    return jnp.sum((pos[:, None] >= ends[None, :]).astype(jnp.int32), axis=1)


def block_grad(queries_blk, keys_blk, values_blk, up_blk, seg):
    rows = queries_blk.shape[0]
    group = HEADS // KV_HEADS
    scale = 1.0 / HEAD_DIM**0.5
    qh = queries_blk.reshape(rows, KV_HEADS, group, HEAD_DIM)
    kh = keys_blk.reshape(rows, KV_HEADS, HEAD_DIM)
    vh = values_blk.reshape(rows, KV_HEADS, HEAD_DIM)
    uh = up_blk.reshape(rows, KV_HEADS, group, HEAD_DIM)
    pos = jnp.arange(rows, dtype=jnp.int32)
    allowed = (seg[:, None] == seg[None, :]) & (pos[None, :] <= pos[:, None])
    scores = jnp.einsum("ikgd,jkd->kgij", qh, kh, preferred_element_type=jnp.float32) * scale
    scores = jnp.where(allowed, scores, jnp.float32(-1e30))
    top = jnp.max(scores, axis=-1, keepdims=True)
    weights = jnp.exp(scores - top)
    probs = weights / jnp.sum(weights, axis=-1, keepdims=True)
    dprobs = jnp.einsum("ikgd,jkd->kgij", uh, vh, preferred_element_type=jnp.float32)
    delta = jnp.sum(probs * dprobs, axis=-1, keepdims=True)
    dscores = (probs * (dprobs - delta) * scale).astype(jnp.bfloat16)
    probs_rounded = probs.astype(jnp.bfloat16)
    dvalues = jnp.einsum("kgij,ikgd->jkd", probs_rounded, uh, preferred_element_type=jnp.float32)
    dkeys = jnp.einsum("kgij,ikgd->jkd", dscores, qh, preferred_element_type=jnp.float32)
    width = KV_HEADS * HEAD_DIM
    return (
        dkeys.reshape(rows, width).astype(jnp.bfloat16),
        dvalues.reshape(rows, width).astype(jnp.bfloat16),
    )


def shards(inputs, queries, top_cotangent, key_weight, value_weight, order, doc_lengths):
    sections = lax.axis_size("section")
    here = lax.axis_index("section")
    key_full, value_full = (
        lax.all_gather(key_weight[0], "fsdp", axis=0, tiled=True),
        lax.all_gather(value_weight[0], "fsdp", axis=0, tiled=True),
    )
    width = key_full.shape[1]
    both = jnp.concatenate([key_full, value_full], axis=1)
    count = inputs.shape[1]
    rows = inputs.shape[2]
    features = inputs.shape[3]

    def attend(micro, upstream):
        acts = inputs[0, micro]
        keyval = jnp.dot(acts, both, preferred_element_type=jnp.float32).astype(jnp.bfloat16)
        seg = segment_ids(doc_lengths[micro, 0], rows)
        dkeys, dvalues = block_grad(
            queries[0, micro], keyval[:, :width], keyval[:, width:], upstream, seg
        )
        return jnp.concatenate([dkeys, dvalues], axis=1)

    def project(dkv, upstream, weights):
        back = lax.dot_general(
            dkv, weights, (((1,), (1,)), ((), ())), preferred_element_type=jnp.float32
        )
        return (upstream.astype(jnp.float32) + back).astype(jnp.bfloat16)

    def compute(micro, upstream):
        return project(attend(micro, upstream), upstream, both)

    def resting(micro, upstream):
        return jnp.zeros_like(upstream)

    def tick(step_count, carry):
        incoming, grads = carry
        position = step_count - (sections - 1 - here)
        active = (position >= 0) & (position < count)
        slot = jnp.clip(position, 0, count - 1)
        micro = order[slot]
        upstream = jnp.where(here == sections - 1, top_cotangent[micro], incoming)
        result = lax.cond(active, compute, resting, micro, upstream)
        incoming = passed_along(result, "section", -1)
        current = grads[0, slot]
        grads = grads.at[0, slot].set(jnp.where(active, result, current))
        return (incoming, grads)

    start = (jnp.zeros((rows, features), jnp.bfloat16), jnp.zeros_like(inputs))
    final_in, grads = lax.fori_loop(0, count + sections - 1, tick, start)
    return grads


def solution(mesh):
    placed = (
        P("section", None, "fsdp", None),
        P("section", None, "fsdp", None),
        P(None, "fsdp", None),
        P("section", "fsdp", None),
        P("section", "fsdp", None),
        P(),
        P(None, "fsdp", None),
    )
    return jax.shard_map(
        shards,
        mesh=mesh,
        in_specs=placed,
        out_specs=P("section", None, "fsdp", None),
        check_vma=False,
    )
```

profile of v0, /device:TPU:0, one launch (start us, length us, event | category | flops | bytes accessed | tf_op | source)
XLA Modules:
  0.0 1064.9 jit_solution(11128387723737905258)
XLA Ops:
  8.0 6.4 copy.30
  14.4 71.1 %all-gather.5.cloned.1.call-done = bf16[1,8192,512]{2,1,0:T(8,128)(2,1)} async-done(((bf16[1,512,512]{2,1,0:T(8,128)(2,1)}), bf16[1,8192,512]{2,1,0:T(8,128)(2,1)}) %all-gather.5.cloned.1.call-update) | async-done | bytes 8388624 | tf_op jit(solution)/shard_map/all_gather | solution.py:55
  85.5 73.3 %all-gather.7.cloned.1.call-done = bf16[1,8192,512]{2,1,0:T(8,128)(2,1)} async-done(((bf16[1,512,512]{2,1,0:T(8,128)(2,1)}), bf16[1,8192,512]{2,1,0:T(8,128)(2,1)}) %all-gather.7.cloned.1.call-update) | async-done | bytes 8388624 | tf_op jit(solution)/shard_map/all_gather | solution.py:56
  158.8 14.0 %pad_maximum_fusion = bf16[8192,1024]{1,0:T(8,128)(2,1)} fusion(bf16[8192,512]{1,0:T(8,128)(2,1)} %bitcast.95, bf16[8192,512]{1,0:T(8,128)(2,1)} %bitcast.94), kind=kLoop, calls=%fused_computation.56 | loop fusion | flops 33554432 | bytes 33554432 | tf_op jit(solution)/shard_map/concatenate | solution.py:59
  176.9 881.2 %while.18 = (s32[]{:T(128)}, bf16[128,8192]{1,0:T(8,128)(2,1)}, bf16[1,2,128,8192]{3,2,1,0:T(8,128)(2,1)}, s32[]{:T(128)}, pred[]{:T(512)}, /*index=5*/s32[2]{0:...) while((s32[]{:T(128)}, bf16[128,8192]{1,0:T(8,128)(2,1)}, ...), condition=%wide.region_9.10_spmd, body=%wide.region_0.9_spmd.sunk | while | flops 5389477376 | bytes 113379856 | solution.py:99
  184.7 43.7 %collective-permute-done = bf16[128,8192]{1,0:T(8,128)(2,1)} collective-permute-done((bf16[128,8192]{1,0:T(8,128)(2,1)}, bf16[128,8192]{1,0:T(8,128)(2,1)}, u32[]{:S(2)}, u32[]{:S(2)}) %collective-permute-start) | collective-permute-done | bytes 2097184 | tf_op jit(solution)/shard_map/while/body/eval_jaxpr/ppermute | solution.py:14
  236.2 42.9 %collective-permute-done = bf16[128,8192]{1,0:T(8,128)(2,1)} collective-permute-done((bf16[128,8192]{1,0:T(8,128)(2,1)}, bf16[128,8192]{1,0:T(8,128)(2,1)}, u32[]{:S(2)}, u32[]{:S(2)}) %collective-permute-start) | collective-permute-done | bytes 2097184 | tf_op jit(solution)/shard_map/while/body/eval_jaxpr/ppermute | solution.py:14
  286.9 42.6 %collective-permute-done = bf16[128,8192]{1,0:T(8,128)(2,1)} collective-permute-done((bf16[128,8192]{1,0:T(8,128)(2,1)}, bf16[128,8192]{1,0:T(8,128)(2,1)}, u32[]{:S(2)}, u32[]{:S(2)}) %collective-permute-start) | collective-permute-done | bytes 2097184 | tf_op jit(solution)/shard_map/while/body/eval_jaxpr/ppermute | solution.py:14
  337.3 42.0 %collective-permute-done = bf16[128,8192]{1,0:T(8,128)(2,1)} collective-permute-done((bf16[128,8192]{1,0:T(8,128)(2,1)}, bf16[128,8192]{1,0:T(8,128)(2,1)}, u32[]{:S(2)}, u32[]{:S(2)}) %collective-permute-start) | collective-permute-done | bytes 2097184 | tf_op jit(solution)/shard_map/while/body/eval_jaxpr/ppermute | solution.py:14
  387.1 41.1 %collective-permute-done = bf16[128,8192]{1,0:T(8,128)(2,1)} collective-permute-done((bf16[128,8192]{1,0:T(8,128)(2,1)}, bf16[128,8192]{1,0:T(8,128)(2,1)}, u32[]{:S(2)}, u32[]{:S(2)}) %collective-permute-start) | collective-permute-done | bytes 2097184 | tf_op jit(solution)/shard_map/while/body/eval_jaxpr/ppermute | solution.py:14
  435.9 40.1 %collective-permute-done = bf16[128,8192]{1,0:T(8,128)(2,1)} collective-permute-done((bf16[128,8192]{1,0:T(8,128)(2,1)}, bf16[128,8192]{1,0:T(8,128)(2,1)}, u32[]{:S(2)}, u32[]{:S(2)}) %collective-permute-start) | collective-permute-done | bytes 2097184 | tf_op jit(solution)/shard_map/while/body/eval_jaxpr/ppermute | solution.py:14
  483.8 381.6 %collective-permute-done = bf16[128,8192]{1,0:T(8,128)(2,1)} collective-permute-done((bf16[128,8192]{1,0:T(8,128)(2,1)}, bf16[128,8192]{1,0:T(8,128)(2,1)}, u32[]{:S(2)}, u32[]{:S(2)}) %collective-permute-start) | collective-permute-done | bytes 2097184 | tf_op jit(solution)/shard_map/while/body/eval_jaxpr/ppermute | solution.py:14
  865.4 50.7 %conditional.2 = (bf16[128,8192]{1,0:T(8,128)(2,1)}) conditional(s32[]{:T(128)} %convert_element_type.81, () %tuple.62, (pred[]{:T(512)}, s32[2]{0:T(128)S(1)}, s32[]{:T(128)}, bf16[2,128,8192]{2,1,0:T(8,128)(2,1)}, bf16[128,8192]{1,0:T(8,128)(2,1)}, /*index=5*/bf16[1,2,128,8192]{2,3,1,0:T(8,128)(2,1)}, s32[2,1,4]{2,1,0:T(1,128)S(1)}, ...), branch_computations={%region_1.1_spmd, %region_2.7_spmd} | conditional | flops 5387380224 | bytes 94504120 | solution.py:92
  868.2 8.7 fusion.17
  887.5 4.3 fusion.33
  891.8 8.0 fusion.24
  903.4 12.8 %fusion.2 = bf16[128,8192]{1,0:T(8,128)(2,1)} fusion(bf16[8192,1024]{1,0:T(8,128)(2,1)} %get-tuple-element.350, bf16[128,8192]{1,0:T(8,128)(2,1)S(1)} %bitcast_select_fusion.4, bf16[128,512]{0,1:T(8,128)(2,1)S(1)} %bitcast.97, bf16[128,512]{0,1:T(8,128)(2,1)S(1)} %bitcast.96), kind=kOutput, calls=%fused_computation.3 | convolution fusion | flops 2151153664 | bytes 21233664 | tf_op jit(solution)/shard_map/while/body/eval_jaxpr/cond/branch_1_fun/dot_general | solution.py:74
  924.0 38.5 %collective-permute-done = bf16[128,8192]{1,0:T(8,128)(2,1)} collective-permute-done((bf16[128,8192]{1,0:T(8,128)(2,1)}, bf16[128,8192]{1,0:T(8,128)(2,1)}, u32[]{:S(2)}, u32[]{:S(2)}) %collective-permute-start) | collective-permute-done | bytes 2097184 | tf_op jit(solution)/shard_map/while/body/eval_jaxpr/ppermute | solution.py:14
  962.5 50.7 %conditional.2 = (bf16[128,8192]{1,0:T(8,128)(2,1)}) conditional(s32[]{:T(128)} %convert_element_type.81, () %tuple.62, (pred[]{:T(512)}, s32[2]{0:T(128)S(1)}, s32[]{:T(128)}, bf16[2,128,8192]{2,1,0:T(8,128)(2,1)}, bf16[128,8192]{1,0:T(8,128)(2,1)}, /*index=5*/bf16[1,2,128,8192]{2,3,1,0:T(8,128)(2,1)}, s32[2,1,4]{2,1,0:T(1,128)S(1)}, ...), branch_computations={%region_1.1_spmd, %region_2.7_spmd} | conditional | flops 5387380224 | bytes 94504120 | solution.py:92
  965.3 8.7 fusion.17
  984.6 4.3 fusion.33
  988.9 8.0 fusion.24
  1000.5 12.8 %fusion.2 = bf16[128,8192]{1,0:T(8,128)(2,1)} fusion(bf16[8192,1024]{1,0:T(8,128)(2,1)} %get-tuple-element.350, bf16[128,8192]{1,0:T(8,128)(2,1)S(1)} %bitcast_select_fusion.4, bf16[128,512]{0,1:T(8,128)(2,1)S(1)} %bitcast.97, bf16[128,512]{0,1:T(8,128)(2,1)S(1)} %bitcast.96), kind=kOutput, calls=%fused_computation.3 | convolution fusion | flops 2151153664 | bytes 21233664 | tf_op jit(solution)/shard_map/while/body/eval_jaxpr/cond/branch_1_fun/dot_general | solution.py:74
  1021.1 37.0 %collective-permute-done = bf16[128,8192]{1,0:T(8,128)(2,1)} collective-permute-done((bf16[128,8192]{1,0:T(8,128)(2,1)}, bf16[128,8192]{1,0:T(8,128)(2,1)}, u32[]{:S(2)}, u32[]{:S(2)}) %collective-permute-start) | collective-permute-done | bytes 2097184 | tf_op jit(solution)/shard_map/while/body/eval_jaxpr/ppermute | solution.py:14
  (92 shorter events, 115.8 us)
Async XLA Ops:
  6.5 78.9 %all-gather.5.cloned.1.call-start = ((), (), s32[]{:S(2)}) async-start(), calls=%async_computation | async-start | bytes 8912896 | tf_op jit(solution)/shard_map/all_gather | solution.py:55
  7.3 151.5 %all-gather.7.cloned.1.call-start = ((), (), s32[]{:S(2)}) async-start(), calls=%async_computation.1 | async-start | bytes 8912896 | tf_op jit(solution)/shard_map/all_gather | solution.py:56
  172.8 4.1 copy-start.1
  172.8 4.1 copy-start.2
  172.8 4.1 copy-start.3
  178.4 50.0 %collective-permute-start = (bf16[128,8192]{1,0:T(8,128)(2,1)}, bf16[128,8192]{1,0:T(8,128)(2,1)}, u32[]{:S(2)}, u32[]{:S(2)}) collective-permute-start(bf16[128,8192]{1,0:T(8,128)(2,1)} %get-tuple-element.528), channel_id=1, source_target_pairs={{16,0},{32,16},{48,32},{64,48},{80,64},{96,80},{112,96},{17,1},{33... | collective-permute-start | bytes 6291464 | tf_op jit(solution)/shard_map/while/body/eval_jaxpr/ppermute | solution.py:14
  229.9 49.2 %collective-permute-start = (bf16[128,8192]{1,0:T(8,128)(2,1)}, bf16[128,8192]{1,0:T(8,128)(2,1)}, u32[]{:S(2)}, u32[]{:S(2)}) collective-permute-start(bf16[128,8192]{1,0:T(8,128)(2,1)} %get-tuple-element.528), channel_id=1, source_target_pairs={{16,0},{32,16},{48,32},{64,48},{80,64},{96,80},{112,96},{17,1},{33... | collective-permute-start | bytes 6291464 | tf_op jit(solution)/shard_map/while/body/eval_jaxpr/ppermute | solution.py:14
  280.7 48.9 %collective-permute-start = (bf16[128,8192]{1,0:T(8,128)(2,1)}, bf16[128,8192]{1,0:T(8,128)(2,1)}, u32[]{:S(2)}, u32[]{:S(2)}) collective-permute-start(bf16[128,8192]{1,0:T(8,128)(2,1)} %get-tuple-element.528), channel_id=1, source_target_pairs={{16,0},{32,16},{48,32},{64,48},{80,64},{96,80},{112,96},{17,1},{33... | collective-permute-start | bytes 6291464 | tf_op jit(solution)/shard_map/while/body/eval_jaxpr/ppermute | solution.py:14
  331.1 48.2 %collective-permute-start = (bf16[128,8192]{1,0:T(8,128)(2,1)}, bf16[128,8192]{1,0:T(8,128)(2,1)}, u32[]{:S(2)}, u32[]{:S(2)}) collective-permute-start(bf16[128,8192]{1,0:T(8,128)(2,1)} %get-tuple-element.528), channel_id=1, source_target_pairs={{16,0},{32,16},{48,32},{64,48},{80,64},{96,80},{112,96},{17,1},{33... | collective-permute-start | bytes 6291464 | tf_op jit(solution)/shard_map/while/body/eval_jaxpr/ppermute | solution.py:14
  380.8 47.3 %collective-permute-start = (bf16[128,8192]{1,0:T(8,128)(2,1)}, bf16[128,8192]{1,0:T(8,128)(2,1)}, u32[]{:S(2)}, u32[]{:S(2)}) collective-permute-start(bf16[128,8192]{1,0:T(8,128)(2,1)} %get-tuple-element.528), channel_id=1, source_target_pairs={{16,0},{32,16},{48,32},{64,48},{80,64},{96,80},{112,96},{17,1},{33... | collective-permute-start | bytes 6291464 | tf_op jit(solution)/shard_map/while/body/eval_jaxpr/ppermute | solution.py:14
  429.7 46.4 %collective-permute-start = (bf16[128,8192]{1,0:T(8,128)(2,1)}, bf16[128,8192]{1,0:T(8,128)(2,1)}, u32[]{:S(2)}, u32[]{:S(2)}) collective-permute-start(bf16[128,8192]{1,0:T(8,128)(2,1)} %get-tuple-element.528), channel_id=1, source_target_pairs={{16,0},{32,16},{48,32},{64,48},{80,64},{96,80},{112,96},{17,1},{33... | collective-permute-start | bytes 6291464 | tf_op jit(solution)/shard_map/while/body/eval_jaxpr/ppermute | solution.py:14
  477.6 387.9 %collective-permute-start = (bf16[128,8192]{1,0:T(8,128)(2,1)}, bf16[128,8192]{1,0:T(8,128)(2,1)}, u32[]{:S(2)}, u32[]{:S(2)}) collective-permute-start(bf16[128,8192]{1,0:T(8,128)(2,1)} %get-tuple-element.528), channel_id=1, source_target_pairs={{16,0},{32,16},{48,32},{64,48},{80,64},{96,80},{112,96},{17,1},{33... | collective-permute-start | bytes 6291464 | tf_op jit(solution)/shard_map/while/body/eval_jaxpr/ppermute | solution.py:14
  878.7 3.8 copy-start
  916.1 46.4 %collective-permute-start = (bf16[128,8192]{1,0:T(8,128)(2,1)}, bf16[128,8192]{1,0:T(8,128)(2,1)}, u32[]{:S(2)}, u32[]{:S(2)}) collective-permute-start(bf16[128,8192]{1,0:T(8,128)(2,1)} %get-tuple-element.528), channel_id=1, source_target_pairs={{16,0},{32,16},{48,32},{64,48},{80,64},{96,80},{112,96},{17,1},{33... | collective-permute-start | bytes 6291464 | tf_op jit(solution)/shard_map/while/body/eval_jaxpr/ppermute | solution.py:14
  975.8 3.8 copy-start
  1013.2 44.8 %collective-permute-start = (bf16[128,8192]{1,0:T(8,128)(2,1)}, bf16[128,8192]{1,0:T(8,128)(2,1)}, u32[]{:S(2)}, u32[]{:S(2)}) collective-permute-start(bf16[128,8192]{1,0:T(8,128)(2,1)} %get-tuple-element.528), channel_id=1, source_target_pairs={{16,0},{32,16},{48,32},{64,48},{80,64},{96,80},{112,96},{17,1},{33... | collective-permute-start | bytes 6291464 | tf_op jit(solution)/shard_map/while/body/eval_jaxpr/ppermute | solution.py:14
Sparse Core Ops, SparseCore 0:
  9.8 75.5 all-gather.4
  87.9 70.8 all-gather.6
where the time goes:
time: 1070 us; the launch traced here: 1060 us
  waiting for transfers between devices  855 us (80%)
  matrix products  81.5 us (8%)
  other arithmetic  51.8 us (5%)
  local copies, waits for them, and re-layouts  46.7 us (4%)
  between operations  13.4 us (1%)
  starting transfers between devices  11.6 us (1%)
    ppermute x9, waiting for transfers between devices, passed_along(): lax.ppermute(value, axis, [(source, source + steps) for source in range(i...  710 us
    all_gather x1, waiting for transfers between devices, shards(): lax.all_gather(value_weight[0], 'fsdp', axis=0, tiled=True)  73.3 us
    all_gather x1, waiting for transfers between devices, shards(): lax.all_gather(key_weight[0], 'fsdp', axis=0, tiled=True)  71.1 us
    scatter x9, other arithmetic, tick(): grads = grads.at[0, slot].set(jnp.where(active, result, current))  25.8 us
    dot_general x2, matrix products, project(): lax.dot_general(dkv, weights, (((1,), (1,)), ((), ())), preferred_element...  25.5 us
  transfers between devices with their start and end apart: 11, of which 11 were waited for; matrix products, arithmetic and copies ran while one was open for 5% of the time, Pallas kernels for 0%

commit v1 on v0

v1 whole, which is shorter than its diff:
```python
import functools
import math

import jax
import jax.numpy as jnp
from jax import lax
from jax.experimental import pallas as pl
from jax.experimental.pallas import tpu as pltpu
from jax.sharding import PartitionSpec as P

MESH = pl.DeviceIdType.MESH
HEADS = 64
KV_HEADS = 4
GROUP = HEADS // KV_HEADS
HEAD_DIM = 128
ROWS = 16
LONGEST = 64
WINDOW = LONGEST + ROWS
NT = (((1,), (1,)), ((), ()))


def kernel(
    sections, micros, tokens,
    acts_hbm, q_hbm, top_hbm, kw_hbm, vw_hbm, lens, out_hbm,
    wt, acts, q, up, down, raw, kv_acc, kv, pt, acc,
    load_sem, out_sem, gather_send, gather_recv, chain_send, chain_recv,
):
    section, f = lax.axis_index("section"), lax.axis_index("fsdp")
    z, h, c = f // 4, (f // 2) % 2, f % 2
    shard = raw.shape[1]
    width = raw.shape[2]
    piece = GROUP * HEAD_DIM
    per_micro = tokens // ROWS
    chunks = micros * per_micro

    def index(dz, dh, dc):
        return 4 * ((z + dz + 4) % 4) + 2 * ((h + dh) % 2) + (c + dc) % 2

    z_next, z_prev = (section, index(1, 0, 0)), (section, index(-1, 0, 0))
    x_pair, core_pair = (section, index(0, 1, 0)), (section, index(0, 0, 1))
    onward = ((section + sections - 1) % sections, f)
    before = ((section + 1) % sections, f)

    loads = [
        pltpu.make_async_copy(kw_hbm, raw.at[0], load_sem.at[0]),
        pltpu.make_async_copy(vw_hbm, raw.at[1], load_sem.at[1]),
        pltpu.make_async_copy(acts_hbm, acts, load_sem.at[2]),
        pltpu.make_async_copy(q_hbm, q, load_sem.at[3]),
    ]
    for load in loads:
        load.start()
    load_top = pltpu.make_async_copy(top_hbm, up, load_sem.at[4])

    @pl.when(section == sections - 1)
    def _():
        load_top.start()

    barrier = pltpu.get_barrier_semaphore()
    for device in (z_next, z_prev, x_pair, core_pair, onward, before):
        pl.semaphore_signal(barrier, inc=1, device_id=device, device_id_type=MESH)

    for part in range(2):
        loads[part].wait()
        wt[f, part * width:(part + 1) * width, :] = jnp.transpose(raw[part])
    pl.semaphore_wait(barrier, 6)

    def copy(role, half, owner, device):
        block = wt.at[owner, pl.ds(half * width, width), :]
        return pltpu.make_async_remote_copy(
            src_ref=block, dst_ref=block,
            send_sem=gather_send.at[role, half], recv_sem=gather_recv.at[role, half],
            device_id=device, device_id_type=MESH,
        )

    sent = []

    def send(role, half, owner, device):
        copy(role, half, owner, device).start()
        sent.append((role, half, owner, device))

    def arrive(role, half, owner, device):
        copy(role, half, owner, device).wait_recv()

    places = [(0, 0), (-1, 0), (1, 0), (0, 1), (2, 0), (-1, 1), (1, 1), (2, 1)]
    own = index(0, 0, 0)

    def to_core(place, half):
        send(7 + place, half, index(*places[place], 0), core_pair)

    def from_core(place):
        for half in range(2):
            arrive(7 + place, half, index(*places[place], 1), core_pair)

    def add_keyval(dz, dh):
        def one(dc, carry):
            owner = index(dz, dh, dc)
            cols = pl.ds(pl.multiple_of(owner * shard, shard), shard)
            kv_acc[...] += lax.dot_general(
                acts[:, cols], wt[owner], NT, preferred_element_type=jnp.float32
            )
            return carry

        lax.fori_loop(0, 2, one, 0)

    for half in range(2):
        send(0, half, own, z_next)
        send(1, half, own, z_prev)
        send(2, half, own, x_pair)
    for half in range(2):
        to_core(0, half)
    kv_acc[...] = jnp.zeros_like(kv_acc)
    acc[...] = jnp.zeros_like(acc)
    loads[2].wait()
    loads[3].wait()
    from_core(0)
    add_keyval(0, 0)

    for half in range(2):
        arrive(0, half, index(-1, 0, 0), z_prev)
        if half == 0:
            send(3, half, index(-1, 0, 0), z_next)
        to_core(1, half)
        arrive(1, half, index(1, 0, 0), z_next)
        if half == 1:
            send(3, half, index(1, 0, 0), z_prev)
        to_core(2, half)
        arrive(2, half, index(0, 1, 0), x_pair)
        send(4, half, index(0, 1, 0), z_next)
        send(5, half, index(0, 1, 0), z_prev)
        to_core(3, half)
    for place in (1, 2, 3):
        from_core(place)
        add_keyval(*places[place])
    for half in range(2):
        arrive(3, half, index(2, 0, 0), z_prev if half == 0 else z_next)
        send(6, half, index(2, 0, 0), x_pair)
        to_core(4, half)
        if half == 1:
            from_core(4)
            add_keyval(*places[4])
        arrive(4, half, index(-1, 1, 0), z_prev)
        to_core(5, half)
        arrive(5, half, index(1, 1, 0), z_next)
        to_core(6, half)
    for place in (5, 6):
        from_core(place)
        add_keyval(*places[place])
    for half in range(2):
        arrive(6, half, index(2, 1, 0), x_pair)
        to_core(7, half)
    from_core(7)
    add_keyval(*places[7])
    kv[...] = kv_acc[...].astype(jnp.bfloat16)

    def place_of(chunk):
        micro = chunk // per_micro
        first = tokens - ROWS - ROWS * (chunk % per_micro)
        base = micro * tokens
        row = pl.multiple_of(base + first, ROWS)
        low = jnp.maximum(first - LONGEST, 0)
        return micro, first, row, low, pl.multiple_of(base + low, ROWS)

    def stacked(ref, row, k):
        return jnp.concatenate(
            [
                ref[pl.ds(row, ROWS), (GROUP * k + g) * HEAD_DIM:(GROUP * k + g + 1) * HEAD_DIM]
                for g in range(GROUP)
            ],
            axis=0,
        )

    def scores(chunk):
        micro, first, row, low, low_row = place_of(chunk)
        end0 = lens[micro, 0]
        end1 = end0 + lens[micro, 1]
        end2 = end1 + lens[micro, 2]
        shape = (WINDOW, GROUP * ROWS)
        i = first + lax.broadcasted_iota(jnp.int32, (1, shape[1]), 1) % ROWS
        begin = jnp.where(i >= end2, end2, jnp.where(i >= end1, end1, jnp.where(i >= end0, end0, 0)))
        j = low + lax.broadcasted_iota(jnp.int32, shape, 0)
        allowed = (j >= begin) & (j <= i)
        for k in range(KV_HEADS):
            keys = kv[pl.ds(low_row, WINDOW), k * HEAD_DIM:(k + 1) * HEAD_DIM]
            s = lax.dot_general(keys, stacked(q, row, k), NT, preferred_element_type=jnp.float32)
            s = jnp.where(allowed, s * (math.log2(math.e) / HEAD_DIM**0.5), -1e30)
            weights = jnp.exp2(s - jnp.max(s, axis=0, keepdims=True))
            probs = weights / jnp.sum(weights, axis=0, keepdims=True)
            pt[k] = probs.astype(jnp.bfloat16)

    def hop(chunk, row, k):
        block = pl.ds(row, ROWS), pl.ds(k * piece, piece)
        return pltpu.make_async_remote_copy(
            src_ref=down.at[block], dst_ref=up.at[block],
            send_sem=chain_send.at[chunk, k], recv_sem=chain_recv.at[chunk, k],
            device_id=onward, device_id_type=MESH,
        )

    def result(chunk, row):
        block = pl.ds(row, ROWS)
        return pltpu.make_async_copy(down.at[block], out_hbm.at[block], out_sem.at[chunk])

    def step(chunk, carry):
        micro, first, row, low, low_row = place_of(chunk)
        for k in range(KV_HEADS):

            @pl.when(section < sections - 1)
            def _():
                hop(chunk, row, k).wait_recv()

            heads = slice(k * HEAD_DIM, (k + 1) * HEAD_DIM)
            dv_heads = slice(width + k * HEAD_DIM, width + (k + 1) * HEAD_DIM)
            u = stacked(up, row, k)
            values = kv[pl.ds(low_row, WINDOW), dv_heads]
            dprobs = lax.dot_general(values, u, NT, preferred_element_type=jnp.float32)
            probs_rounded = pt[k]
            probs = probs_rounded.astype(jnp.float32)
            delta = jnp.sum(probs * dprobs, axis=0, keepdims=True)
            dscores = (probs * (dprobs - delta)).astype(jnp.bfloat16)
            acc[pl.ds(low_row, WINDOW), heads] += jnp.dot(
                dscores, stacked(q, row, k), preferred_element_type=jnp.float32
            )
            acc[pl.ds(low_row, WINDOW), dv_heads] += jnp.dot(
                probs_rounded, u, preferred_element_type=jnp.float32
            )
        dkeys = acc[pl.ds(row, ROWS), :width] * (1.0 / HEAD_DIM**0.5)
        dkv = jnp.concatenate([dkeys, acc[pl.ds(row, ROWS), width:]], axis=1).astype(jnp.bfloat16)
        for k in range(KV_HEADS):
            for owner in range(k * piece // shard, (k + 1) * piece // shard):
                cols = slice(owner * shard, (owner + 1) * shard)
                back = jnp.dot(dkv, wt[owner], preferred_element_type=jnp.float32)
                down[pl.ds(row, ROWS), cols] = (
                    up[pl.ds(row, ROWS), cols].astype(jnp.float32) + back
                ).astype(jnp.bfloat16)

            @pl.when(section > 0)
            def _():
                hop(chunk, row, k).start()

        result(chunk, row).start()

        @pl.when(chunk < chunks - 1)
        def _():
            scores(chunk + 1)

        return carry

    scores(0)

    @pl.when(section == sections - 1)
    def _():
        load_top.wait()

    lax.fori_loop(0, chunks, step, 0)

    def finish(chunk, carry):
        row = place_of(chunk)[2]
        result(chunk, row).wait()

        @pl.when(section > 0)
        def _():
            for k in range(KV_HEADS):
                hop(chunk, row, k).wait_send()

        return carry

    lax.fori_loop(0, chunks, finish, 0)
    for item in sent:
        copy(*item).wait_send()


def shards(inputs, queries, top_cotangent, key_weight, value_weight, order, doc_lengths):
    sections, fsdp = lax.axis_size("section"), lax.axis_size("fsdp")
    _, micros, tokens, features = inputs.shape
    shard, width = key_weight.shape[1:]
    rows = micros * tokens
    chunks = rows // ROWS
    bf16, f32 = jnp.bfloat16, jnp.float32
    hbm = pl.BlockSpec(memory_space=pl.ANY)
    grads = pl.pallas_call(
        functools.partial(kernel, sections, micros, tokens),
        out_shape=jax.ShapeDtypeStruct((rows, features), bf16),
        in_specs=[hbm] * 5 + [pl.BlockSpec(memory_space=pltpu.SMEM)],
        out_specs=hbm,
        scratch_shapes=[
            pltpu.VMEM((fsdp, 2 * width, shard), bf16),
            pltpu.VMEM((rows, features), bf16),
            pltpu.VMEM((rows, features), bf16),
            pltpu.VMEM((rows, features), bf16),
            pltpu.VMEM((rows, features), bf16),
            pltpu.VMEM((2, shard, width), bf16),
            pltpu.VMEM((rows, 2 * width), f32),
            pltpu.VMEM((rows, 2 * width), bf16),
            pltpu.VMEM((KV_HEADS, WINDOW, GROUP * ROWS), bf16),
            pltpu.VMEM((rows, 2 * width), f32),
            pltpu.SemaphoreType.DMA((5,)),
            pltpu.SemaphoreType.DMA((chunks,)),
            pltpu.SemaphoreType.DMA((15, 2)),
            pltpu.SemaphoreType.DMA((15, 2)),
            pltpu.SemaphoreType.DMA((chunks, KV_HEADS)),
            pltpu.SemaphoreType.DMA((chunks, KV_HEADS)),
        ],
        compiler_params=pltpu.CompilerParams(
            collective_id=0, has_side_effects=True, vmem_limit_bytes=52 << 20
        ),
        name="chain",
    )(
        inputs.reshape(rows, features),
        queries.reshape(rows, features),
        top_cotangent.reshape(rows, features),
        key_weight[0],
        value_weight[0],
        doc_lengths.reshape(micros, -1),
    )
    grads = grads.reshape(micros, tokens, features)
    return jnp.stack([lax.dynamic_index_in_dim(grads, order[k], 0, False) for k in range(micros)])[None]


def solution(mesh):
    placed = (
        P("section", None, "fsdp", None),
        P("section", None, "fsdp", None),
        P(None, "fsdp", None),
        P("section", "fsdp", None),
        P("section", "fsdp", None),
        P(),
        P(None, "fsdp", None),
    )
    return jax.shard_map(
        shards,
        mesh=mesh,
        in_specs=placed,
        out_specs=P("section", None, "fsdp", None),
        check_vma=False,
    )
```

time: 1070 us -> 232 us (0.22)
  waiting for transfers between devices: 855 us -> 0 us
  Pallas kernels: 0 us -> 218 us
  matrix products: 81.5 us -> 0 us
  other arithmetic: 51.8 us -> 2.38 us
  local copies, waits for them, and re-layouts: 46.7 us -> 6.58 us
  starting transfers between devices: 11.6 us -> 0 us
    ppermute x9 -> x0, waiting for transfers between devices: 710 us -> none  [passed_along(): lax.ppermute(value, axis, [(source, source + steps) for source in range(i...]
    pallas_call x0 -> x1, Pallas kernels: none -> 218 us  [shards(): pl.pallas_call(functools.partial(kernel, sections, micros, tokens), out_s...]
    all_gather x2 -> x0, waiting for transfers between devices: 144 us -> none  [the longest x1 73.3 us: shards(): lax.all_gather(value_weight[0], 'fsdp', axis=0, tiled=True)]
    dot_general x10 -> x0, matrix products: 74.7 us -> none  [the longest x2 25.5 us: project(): lax.dot_general(dkv, weights, (((1,), (1,)), ((), ())), preferred_element...]
    scatter x9 -> x0, other arithmetic: 25.8 us -> none  [tick(): grads = grads.at[0, slot].set(jnp.where(active, result, current))]
    dynamic_slice x13 -> x1, local copies, waits for them, and re-layouts: 20.4 us -> 2.5 us  [shards(): lax.dynamic_index_in_dim(grads, order[k], 0, False)]
    concatenate x1 -> x0, other arithmetic: 14 us -> none  [shards(): both = jnp.concatenate([key_full, value_full], axis=1)]
    another operation x10 -> x0, local copies, waits for them, and re-layouts: 12.3 us -> none
  transfers between devices with their start and end apart: 11 -> 0, of which waited for: 11 -> 0; matrix products, arithmetic and copies ran while one was open for 5% -> 0% of each run, Pallas kernels for 0% -> 0%
where the time goes in v1:
time: 232 us; the launch traced here: 231 us
  Pallas kernels  218 us (94%)
  local copies, waits for them, and re-layouts  6.58 us (3%)
  between operations  3.82 us (2%)
  other arithmetic  2.38 us (1%)
    pallas_call x1, Pallas kernels, shards(): pl.pallas_call(functools.partial(kernel, sections, micros, tokens), out_s...  218 us

profile of v1, /device:TPU:0, one launch (start us, length us, event | category | flops | bytes accessed | tf_op | source)
XLA Modules:
  0.0 231.3 jit_solution(997052078037760440)
XLA Ops:
  0.0 1.3 fusion
  5.1 0.0 copy-start
  5.1 1.0 copy-done
  6.2 0.0 copy-start.1
  6.2 1.0 copy-done.1
  7.2 0.0 copy-start.2
  7.2 0.7 copy-done.2
  7.9 218.5 %chain.1 = bf16[256,8192]{1,0:T(8,128)(2,1)} custom-call(bf16[256,8192]{1,0:T(8,128)(2,1)} %bitcast.15, bf16[256,8192]{1,0:T(8,128)(2,1)} %bitcast.16, bf16[256,8192]{1,0:T(8,128)(2,1)} %bitcast.17, bf16[512,512]{1,0:T(8,128)(2,1)S(1)} %bitcast.11, bf16[512,512]{1,0:T(8,128)(2,1)S(1)} %bitcast.12, s32[2,4]{1,0:T(2,128)S(1)} %bitcast.13), custom_call_target="tpu_custom_call" | custom-call | tf_op jit(solution)/shard_map/chain/pallas_call | solution.py:279
  226.4 2.5 %constant_dynamic-slice_fusion.1 = (bf16[1,128,8192]{2,1,0:T(8,128)(2,1)S(1)}, bf16[1,128,8192]{2,1,0:T(8,128)(2,1)S(1)}) fusion(bf16[2,128,8192]{2,1,0:T(8,128)(2,1)} %bitcast.14, s32[]{:T(128)S(6)} %select_n.7, s32[]{:T(128)S(6)} %select_n.8), kind=kLoop, calls=%fused_computation.2 | loop fusion | bytes 8388616 | tf_op jit(solution)/shard_map/jit(dynamic_index_in_dim)/dynamic_slice | solution.py:315
  228.9 2.4 %maximum_bitcast_fusion = bf16[1,2,128,8192]{3,2,1,0:T(8,128)(2,1)} fusion(bf16[1,128,8192]{2,1,0:T(8,128)(2,1)S(1)} %get-tuple-element.6, bf16[1,128,8192]{2,1,0:T(8,128)(2,1)S(1)} %get-tuple-element.5), kind=kLoop, calls=%fused_computation | loop fusion | flops 2097152 | bytes 8388608 | tf_op jit(solution)/shard_map/broadcast_in_dim | solution.py:315
Async XLA Ops:
  5.1 1.0 copy-start
  6.2 1.0 copy-start.1
  7.2 0.7 copy-start.2

commit v2 on v1

--- a/solution.py
+++ b/solution.py
@@ -21,9 +21,9 @@
 
 def kernel(
     sections, micros, tokens,
-    acts_hbm, q_hbm, top_hbm, kw_hbm, vw_hbm, lens, out_hbm,
-    wt, acts, q, up, down, raw, kv_acc, kv, pt, acc,
-    load_sem, out_sem, gather_send, gather_recv, chain_send, chain_recv,
+    acts_hbm, q_hbm, top_hbm, kw_hbm, vw_hbm, lens, down,
+    wt, acts, q, up, raw, kv_acc, kv, pt, acc,
+    load_sem, gather_send, gather_recv, chain_send, chain_recv,
 ):
     section, f = lax.axis_index("section"), lax.axis_index("fsdp")
     z, h, c = f // 4, (f // 2) % 2, f % 2
@@ -47,13 +47,9 @@
         pltpu.make_async_copy(acts_hbm, acts, load_sem.at[2]),
         pltpu.make_async_copy(q_hbm, q, load_sem.at[3]),
     ]
-    for load in loads:
+    load_top = pltpu.make_async_copy(top_hbm, up, load_sem.at[4])
+    for load in loads[:2]:
         load.start()
-    load_top = pltpu.make_async_copy(top_hbm, up, load_sem.at[4])
-
-    @pl.when(section == sections - 1)
-    def _():
-        load_top.start()
 
     barrier = pltpu.get_barrier_semaphore()
     for device in (z_next, z_prev, x_pair, core_pair, onward, before):
@@ -64,92 +60,94 @@
         wt[f, part * width:(part + 1) * width, :] = jnp.transpose(raw[part])
     pl.semaphore_wait(barrier, 6)
 
-    def copy(role, half, owner, device):
-        block = wt.at[owner, pl.ds(half * width, width), :]
+    places = [(0, 0), (-1, 0), (1, 0), (0, 1), (2, 0), (1, 1), (-1, 1), (2, 1)]
+    third = (2 * width // 3) // 16 * 16
+    parts = [(0, third), (third, third), (2 * third, 2 * width - 2 * third)]
+    from_0, from_1, from_2 = (0, 1, 2), (1, 2, 0), (2, 0, 1)
+
+    def copy(role, part, owner, device):
+        first, size = parts[part]
+        block = wt.at[owner, pl.ds(first, size), :]
         return pltpu.make_async_remote_copy(
             src_ref=block, dst_ref=block,
-            send_sem=gather_send.at[role, half], recv_sem=gather_recv.at[role, half],
+            send_sem=gather_send.at[role, part], recv_sem=gather_recv.at[role, part],
             device_id=device, device_id_type=MESH,
         )
 
     sent = []
 
-    def send(role, half, owner, device):
-        copy(role, half, owner, device).start()
-        sent.append((role, half, owner, device))
-
-    def arrive(role, half, owner, device):
-        copy(role, half, owner, device).wait_recv()
-
-    places = [(0, 0), (-1, 0), (1, 0), (0, 1), (2, 0), (-1, 1), (1, 1), (2, 1)]
-    own = index(0, 0, 0)
-
-    def to_core(place, half):
-        send(7 + place, half, index(*places[place], 0), core_pair)
-
-    def from_core(place):
-        for half in range(2):
-            arrive(7 + place, half, index(*places[place], 1), core_pair)
-
-    def add_keyval(dz, dh):
-        def one(dc, carry):
-            owner = index(dz, dh, dc)
+    def send(role, part, place, device):
+        owner = index(*places[place], 0)
+        copy(role, part, owner, device).start()
+        sent.append((role, part, owner, device))
+
+    def arrive(role, part, place, device, dc=0):
+        copy(role, part, index(*places[place], dc), device).wait_recv()
+
+    def to_core(place, part):
+        send(8 + place, part, place, core_pair)
+
+    def add_keyval(place):
+        for dc in range(2):
+            if dc == 1:
+                for part in from_0:
+                    arrive(8 + place, part, place, core_pair, 1)
+            owner = index(*places[place], dc)
             cols = pl.ds(pl.multiple_of(owner * shard, shard), shard)
             kv_acc[...] += lax.dot_general(
                 acts[:, cols], wt[owner], NT, preferred_element_type=jnp.float32
             )
-            return carry
-
-        lax.fori_loop(0, 2, one, 0)
-
-    for half in range(2):
-        send(0, half, own, z_next)
-        send(1, half, own, z_prev)
-        send(2, half, own, x_pair)
-    for half in range(2):
-        to_core(0, half)
+
+    for i in range(3):
+        send(0, from_2[i], 0, z_next)
+        send(1, from_0[i], 0, z_prev)
+        send(2, from_1[i], 0, x_pair)
+    for part in from_0:
+        to_core(0, part)
+    for load in loads[2:]:
+        load.start()
+
+    @pl.when(section == sections - 1)
+    def _():
+        load_top.start()
+
     kv_acc[...] = jnp.zeros_like(kv_acc)
     acc[...] = jnp.zeros_like(acc)
-    loads[2].wait()
-    loads[3].wait()
-    from_core(0)
-    add_keyval(0, 0)
-
-    for half in range(2):
-        arrive(0, half, index(-1, 0, 0), z_prev)
-        if half == 0:
-            send(3, half, index(-1, 0, 0), z_next)
-        to_core(1, half)
-        arrive(1, half, index(1, 0, 0), z_next)
-        if half == 1:
-            send(3, half, index(1, 0, 0), z_prev)
-        to_core(2, half)
-        arrive(2, half, index(0, 1, 0), x_pair)
-        send(4, half, index(0, 1, 0), z_next)
-        send(5, half, index(0, 1, 0), z_prev)
-        to_core(3, half)
-    for place in (1, 2, 3):
-        from_core(place)
-        add_keyval(*places[place])
-    for half in range(2):
-        arrive(3, half, index(2, 0, 0), z_prev if half == 0 else z_next)
-        send(6, half, index(2, 0, 0), x_pair)
-        to_core(4, half)
-        if half == 1:
-            from_core(4)
-            add_keyval(*places[4])
-        arrive(4, half, index(-1, 1, 0), z_prev)
-        to_core(5, half)
-        arrive(5, half, index(1, 1, 0), z_next)
-        to_core(6, half)
-    for place in (5, 6):
-        from_core(place)
-        add_keyval(*places[place])
-    for half in range(2):
-        arrive(6, half, index(2, 1, 0), x_pair)
-        to_core(7, half)
-    from_core(7)
-    add_keyval(*places[7])
+    for i in range(3):
+        arrive(0, from_2[i], 1, z_prev)
+        send(3, from_2[i], 1, z_next)
+        if i > 0:
+            send(4, from_0[i - 1], 1, x_pair)
+        arrive(2, from_1[i], 3, x_pair)
+        send(5, from_1[i], 3, z_prev)
+        arrive(1, from_0[i], 2, z_next)
+        to_core(1, from_2[i])
+        to_core(3, from_1[i])
+        to_core(2, from_0[i])
+    send(4, from_0[2], 1, x_pair)
+    for load in loads[2:]:
+        load.wait()
+    for place in (0, 1, 3, 2):
+        add_keyval(place)
+    for i in range(3):
+        arrive(4, from_0[i], 6, x_pair)
+        if i == 0:
+            send(6, 0, 6, z_next)
+        arrive(5, from_1[i], 5, z_next)
+        if i == 0:
+            send(6, 1, 5, z_prev)
+        arrive(3, from_2[i], 4, z_prev)
+        if i == 0:
+            send(6, 2, 4, x_pair)
+        to_core(6, from_0[i])
+        to_core(5, from_1[i])
+        to_core(4, from_2[i])
+    for place in (6, 5, 4):
+        add_keyval(place)
+    for part, device in zip(from_0, (z_prev, z_next, x_pair)):
+        arrive(6, part, 7, device)
+        to_core(7, part)
+    add_keyval(7)
     kv[...] = kv_acc[...].astype(jnp.bfloat16)
 
     def place_of(chunk):
@@ -171,9 +169,9 @@
 
     def scores(chunk):
         micro, first, row, low, low_row = place_of(chunk)
-        end0 = lens[micro, 0]
-        end1 = end0 + lens[micro, 1]
-        end2 = end1 + lens[micro, 2]
+        end0 = lens[micro, 0, 0]
+        end1 = end0 + lens[micro, 0, 1]
+        end2 = end1 + lens[micro, 0, 2]
         shape = (WINDOW, GROUP * ROWS)
         i = first + lax.broadcasted_iota(jnp.int32, (1, shape[1]), 1) % ROWS
         begin = jnp.where(i >= end2, end2, jnp.where(i >= end1, end1, jnp.where(i >= end0, end0, 0)))
@@ -194,10 +192,6 @@
             send_sem=chain_send.at[chunk, k], recv_sem=chain_recv.at[chunk, k],
             device_id=onward, device_id_type=MESH,
         )
-
-    def result(chunk, row):
-        block = pl.ds(row, ROWS)
-        return pltpu.make_async_copy(down.at[block], out_hbm.at[block], out_sem.at[chunk])
 
     def step(chunk, carry):
         micro, first, row, low, low_row = place_of(chunk)
@@ -236,8 +230,6 @@
             def _():
                 hop(chunk, row, k).start()
 
-        result(chunk, row).start()
-
         @pl.when(chunk < chunks - 1)
         def _():
             scores(chunk + 1)
@@ -254,8 +246,6 @@
 
     def finish(chunk, carry):
         row = place_of(chunk)[2]
-        result(chunk, row).wait()
-
         @pl.when(section > 0)
         def _():
             for k in range(KV_HEADS):
@@ -266,6 +256,23 @@
     lax.fori_loop(0, chunks, finish, 0)
     for item in sent:
         copy(*item).wait_send()
+
+
+def place_micros(order, grads, out, sem):
+    _, micros, tokens, _ = out.shape
+
+    def copies():
+        for k in range(micros):
+            for i in range(tokens // ROWS):
+                row = pl.multiple_of(order[k] * tokens + i * ROWS, ROWS)
+                yield pltpu.make_async_copy(
+                    grads.at[pl.ds(row, ROWS)], out.at[0, k, pl.ds(i * ROWS, ROWS)], sem.at[k, i]
+                )
+
+    for copy in copies():
+        copy.start()
+    for copy in copies():
+        copy.wait()
 
 
 def shards(inputs, queries, top_cotangent, key_weight, value_weight, order, doc_lengths):
@@ -275,15 +282,14 @@
     rows = micros * tokens
     chunks = rows // ROWS
     bf16, f32 = jnp.bfloat16, jnp.float32
-    hbm = pl.BlockSpec(memory_space=pl.ANY)
+    hbm, vmem = pl.BlockSpec(memory_space=pl.ANY), pl.BlockSpec(memory_space=pltpu.VMEM)
     grads = pl.pallas_call(
         functools.partial(kernel, sections, micros, tokens),
-        out_shape=jax.ShapeDtypeStruct((rows, features), bf16),
+        out_shape=pltpu.VMEM((rows, features), bf16),
         in_specs=[hbm] * 5 + [pl.BlockSpec(memory_space=pltpu.SMEM)],
-        out_specs=hbm,
+        out_specs=vmem,
         scratch_shapes=[
             pltpu.VMEM((fsdp, 2 * width, shard), bf16),
-            pltpu.VMEM((rows, features), bf16),
             pltpu.VMEM((rows, features), bf16),
             pltpu.VMEM((rows, features), bf16),
             pltpu.VMEM((rows, features), bf16),
@@ -293,14 +299,13 @@
             pltpu.VMEM((KV_HEADS, WINDOW, GROUP * ROWS), bf16),
             pltpu.VMEM((rows, 2 * width), f32),
             pltpu.SemaphoreType.DMA((5,)),
-            pltpu.SemaphoreType.DMA((chunks,)),
-            pltpu.SemaphoreType.DMA((15, 2)),
-            pltpu.SemaphoreType.DMA((15, 2)),
+            pltpu.SemaphoreType.DMA((16, 3)),
+            pltpu.SemaphoreType.DMA((16, 3)),
             pltpu.SemaphoreType.DMA((chunks, KV_HEADS)),
             pltpu.SemaphoreType.DMA((chunks, KV_HEADS)),
         ],
         compiler_params=pltpu.CompilerParams(
-            collective_id=0, has_side_effects=True, vmem_limit_bytes=52 << 20
+            collective_id=0, has_side_effects=True, vmem_limit_bytes=56 << 20
         ),
         name="chain",
     )(
@@ -309,10 +314,17 @@
         top_cotangent.reshape(rows, features),
         key_weight[0],
         value_weight[0],
-        doc_lengths.reshape(micros, -1),
+        doc_lengths,
     )
-    grads = grads.reshape(micros, tokens, features)
-    return jnp.stack([lax.dynamic_index_in_dim(grads, order[k], 0, False) for k in range(micros)])[None]
+    return pl.pallas_call(
+        place_micros,
+        out_shape=jax.ShapeDtypeStruct((1, micros, tokens, features), bf16),
+        in_specs=[pl.BlockSpec(memory_space=pltpu.SMEM), vmem],
+        out_specs=hbm,
+        scratch_shapes=[pltpu.SemaphoreType.DMA((micros, tokens // ROWS))],
+        compiler_params=pltpu.CompilerParams(vmem_limit_bytes=4 << 20),
+        name="order",
+    )(order, grads)
 
 
 def solution(mesh):

time: 232 us -> 214 us (0.922)
  local copies, waits for them, and re-layouts: 6.58 us -> 0.01 us
  Pallas kernels: 218 us -> 214 us
  between operations: 3.82 us -> 0.02 us
  other arithmetic: 2.38 us -> 0 us
    pallas_call x1, Pallas kernels: 218 us -> 211 us  [shards(): pl.pallas_call(functools.partial(kernel, sections, micros, tokens), out_s...]
    unnamed x6 -> x2, local copies, waits for them, and re-layouts: 2.76 us -> 0.01 us
    pallas_call x0 -> x1, Pallas kernels: none -> 2.68 us  [shards(): pl.pallas_call(place_micros, out_shape=jax.ShapeDtypeStruct((1, micros, t...]
    dynamic_slice x1 -> x0, local copies, waits for them, and re-layouts: 2.5 us -> none  [shards(): lax.dynamic_index_in_dim(grads, order[k], 0, False)]
    broadcast_in_dim x1 -> x0, other arithmetic: 2.38 us -> none  [shards(): jnp.stack([lax.dynamic_index_in_dim(grads, order[k], 0, False) for k in r...]
where the time goes in v2:
time: 214 us
  Pallas kernels  214 us (100%)
    pallas_call x1, Pallas kernels, shards(): pl.pallas_call(functools.partial(kernel, sections, micros, tokens), out_s...  211 us

profile of v2, /device:TPU:0, one launch (start us, length us, event | category | flops | bytes accessed | tf_op | source)
XLA Modules:
  0.0 213.8 jit_solution(17722762551090083465)
XLA Ops:
  0.0 0.0 copy-start
  0.0 211.1 %chain.1.grads = bf16[256,8192]{1,0:T(8,128)(2,1)S(1)} custom-call(bf16[256,8192]{1,0:T(8,128)(2,1)} %bitcast.5, bf16[256,8192]{1,0:T(8,128)(2,1)} %bitcast.6, bf16[256,8192]{1,0:T(8,128)(2,1)} %bitcast.7, bf16[512,512]{1,0:T(8,128)(2,1)} %bitcast.8, bf16[512,512]{1,0:T(8,128)(2,1)} %bitcast.9, s32[2,1,4]{2,1,0:T(1,128)} %lens.1), custom_call_target="tpu_custom_call" | custom-call | tf_op jit(solution)/shard_map/chain/pallas_call | solution.py:286
  211.2 0.0 copy-done
  211.2 2.7 %order.2 = bf16[1,2,128,8192]{3,2,1,0:T(8,128)(2,1)} custom-call(s32[2]{0:T(128)S(1)} %copy-done, bf16[256,8192]{1,0:T(8,128)(2,1)S(1)} %chain.1.grads), custom_call_target="tpu_custom_call" | custom-call | tf_op jit(solution)/shard_map/order/pallas_call | solution.py:319
Async XLA Ops:
  0.0 211.2 %copy-start = (s32[2]{0:T(128)S(1)}, s32[2]{0:T(128)}, u32[]{:S(2)}) copy-start(s32[2]{0:T(128)} %order.3) | copy-start | bytes 28

commit v3 on v2

--- a/solution.py
+++ b/solution.py
@@ -22,7 +22,7 @@
 def kernel(
     sections, micros, tokens,
     acts_hbm, q_hbm, top_hbm, kw_hbm, vw_hbm, lens, down,
-    wt, acts, q, up, raw, kv_acc, kv, pt, acc,
+    wt, relay, acts, q, up, raw, kv_acc, kv, pt, acc,
     load_sem, gather_send, gather_recv, chain_send, chain_recv,
 ):
     section, f = lax.axis_index("section"), lax.axis_index("fsdp")
@@ -51,14 +51,29 @@
     for load in loads[:2]:
         load.start()
 
+    leading, helping = section >= sections - 2, section < 2
+    opposite = (section + 2 * jnp.where(helping, sections // 2 - 1, 1)) % sections
+    facing, across = (opposite, f), (opposite, index(2, 0, 0))
     barrier = pltpu.get_barrier_semaphore()
     for device in (z_next, z_prev, x_pair, core_pair, onward, before):
         pl.semaphore_signal(barrier, inc=1, device_id=device, device_id_type=MESH)
 
+    @pl.when(leading | helping)
+    def _():
+        for device in (facing, across):
+            pl.semaphore_signal(barrier, inc=1, device_id=device, device_id_type=MESH)
+
     for part in range(2):
         loads[part].wait()
         wt[f, part * width:(part + 1) * width, :] = jnp.transpose(raw[part])
-    pl.semaphore_wait(barrier, 6)
+
+    @pl.when(leading | helping)
+    def _():
+        pl.semaphore_wait(barrier, 8)
+
+    @pl.when(jnp.logical_not(leading | helping))
+    def _():
+        pl.semaphore_wait(barrier, 6)
 
     places = [(0, 0), (-1, 0), (1, 0), (0, 1), (2, 0), (1, 1), (-1, 1), (2, 1)]
     third = (2 * width // 3) // 16 * 16
@@ -67,36 +82,57 @@
 
     def copy(role, part, owner, device):
         first, size = parts[part]
-        block = wt.at[owner, pl.ds(first, size), :]
+        rows = pl.ds(first, size)
+        source = relay.at[rows, :] if role == 17 else wt.at[owner, rows, :]
+        target = relay.at[rows, :] if role == 16 else wt.at[owner, rows, :]
         return pltpu.make_async_remote_copy(
-            src_ref=block, dst_ref=block,
+            src_ref=source, dst_ref=target,
             send_sem=gather_send.at[role, part], recv_sem=gather_recv.at[role, part],
             device_id=device, device_id_type=MESH,
         )
 
-    sent = []
-
-    def send(role, part, place, device):
-        owner = index(*places[place], 0)
-        copy(role, part, owner, device).start()
-        sent.append((role, part, owner, device))
+    owners = [index(*place, 0) for place in places]
+    others = [index(*place, 1) for place in places]
+    sent = {"all": [], "leading": [], "following": [], "helping": []}
+
+    def send(role, part, place, device, who="all"):
+        copy(role, part, owners[place], device).start()
+        sent[who].append((role, part, owners[place], device))
 
     def arrive(role, part, place, device, dc=0):
-        copy(role, part, index(*places[place], dc), device).wait_recv()
-
-    def to_core(place, part):
-        send(8 + place, part, place, core_pair)
+        copy(role, part, (others if dc else owners)[place], device).wait_recv()
+
+    def to_core(place, part, who="all"):
+        send(8 + place, part, place, core_pair, who)
 
     def add_keyval(place):
         for dc in range(2):
             if dc == 1:
                 for part in from_0:
                     arrive(8 + place, part, place, core_pair, 1)
-            owner = index(*places[place], dc)
+            owner = (others if dc else owners)[place]
             cols = pl.ds(pl.multiple_of(owner * shard, shard), shard)
             kv_acc[...] += lax.dot_general(
                 acts[:, cols], wt[owner], NT, preferred_element_type=jnp.float32
             )
+
+    for load in loads[2:]:
+        load.start()
+
+    @pl.when(section == sections - 1)
+    def _():
+        load_top.start()
+
+    @pl.when(leading)
+    def _():
+        for part in from_0:
+            send(16, part, 0, across, "leading")
+
+    @pl.when(helping)
+    def _():
+        for part in from_0:
+            arrive(16, part, 0, across)
+            send(17, part, 4, facing, "helping")
 
     for i in range(3):
         send(0, from_2[i], 0, z_next)
@@ -104,49 +140,89 @@
         send(2, from_1[i], 0, x_pair)
     for part in from_0:
         to_core(0, part)
-    for load in loads[2:]:
-        load.start()
-
-    @pl.when(section == sections - 1)
-    def _():
-        load_top.start()
-
     kv_acc[...] = jnp.zeros_like(kv_acc)
     acc[...] = jnp.zeros_like(acc)
     for i in range(3):
         arrive(0, from_2[i], 1, z_prev)
-        send(3, from_2[i], 1, z_next)
-        if i > 0:
-            send(4, from_0[i - 1], 1, x_pair)
+
+        @pl.when(jnp.logical_not(leading))
+        def _():
+            send(3, from_2[i], 1, z_next, "following")
+            if i > 0:
+                send(4, from_0[i - 1], 1, x_pair, "following")
+
         arrive(2, from_1[i], 3, x_pair)
+
+        @pl.when(leading)
+        def _():
+            send(3, from_1[i], 3, z_next, "leading")
+
         send(5, from_1[i], 3, z_prev)
         arrive(1, from_0[i], 2, z_next)
         to_core(1, from_2[i])
         to_core(3, from_1[i])
         to_core(2, from_0[i])
-    send(4, from_0[2], 1, x_pair)
+
+    @pl.when(jnp.logical_not(leading))
+    def _():
+        send(4, from_0[2], 1, x_pair, "following")
+
+    def relayed(part):
+        @pl.when(leading)
+        def _():
+            arrive(17, part, 4, facing)
+            send(4, part, 4, x_pair, "leading")
+            to_core(4, part, "leading")
+
+    relayed(0)
     for load in loads[2:]:
         load.wait()
-    for place in (0, 1, 3, 2):
+    add_keyval(0)
+    add_keyval(1)
+    relayed(1)
+    add_keyval(3)
+    add_keyval(2)
+    relayed(2)
+
+    @pl.when(jnp.logical_not(leading))
+    def _():
+        for i in range(3):
+            arrive(4, from_0[i], 6, x_pair)
+            if i == 0:
+                send(6, 0, 6, z_next, "following")
+            arrive(5, from_1[i], 5, z_next)
+            if i == 0:
+                send(6, 1, 5, z_prev, "following")
+            arrive(3, from_2[i], 4, z_prev)
+            if i == 0:
+                send(6, 2, 4, x_pair, "following")
+            to_core(6, from_0[i], "following")
+            to_core(5, from_1[i], "following")
+            to_core(4, from_2[i], "following")
+
+    @pl.when(leading)
+    def _():
+        for i in range(3):
+            arrive(3, from_1[i], 6, z_prev)
+            to_core(6, from_1[i], "leading")
+            arrive(5, from_1[i], 5, z_next)
+            to_core(5, from_1[i], "leading")
+
+    for place in (4, 6, 5):
         add_keyval(place)
-    for i in range(3):
-        arrive(4, from_0[i], 6, x_pair)
-        if i == 0:
-            send(6, 0, 6, z_next)
-        arrive(5, from_1[i], 5, z_next)
-        if i == 0:
-            send(6, 1, 5, z_prev)
-        arrive(3, from_2[i], 4, z_prev)
-        if i == 0:
-            send(6, 2, 4, x_pair)
-        to_core(6, from_0[i])
-        to_core(5, from_1[i])
-        to_core(4, from_2[i])
-    for place in (6, 5, 4):
-        add_keyval(place)
-    for part, device in zip(from_0, (z_prev, z_next, x_pair)):
-        arrive(6, part, 7, device)
-        to_core(7, part)
+
+    @pl.when(jnp.logical_not(leading))
+    def _():
+        for part, device in zip(from_0, (z_prev, z_next, x_pair)):
+            arrive(6, part, 7, device)
+            to_core(7, part, "following")
+
+    @pl.when(leading)
+    def _():
+        for part in from_0:
+            arrive(4, part, 7, x_pair)
+            to_core(7, part, "leading")
+
     add_keyval(7)
     kv[...] = kv_acc[...].astype(jnp.bfloat16)
 
@@ -195,27 +271,29 @@
 
     def step(chunk, carry):
         micro, first, row, low, low_row = place_of(chunk)
-        for k in range(KV_HEADS):
+        for group in ((0, 1, 2), (3,)):
 
             @pl.when(section < sections - 1)
             def _():
-                hop(chunk, row, k).wait_recv()
-
-            heads = slice(k * HEAD_DIM, (k + 1) * HEAD_DIM)
-            dv_heads = slice(width + k * HEAD_DIM, width + (k + 1) * HEAD_DIM)
-            u = stacked(up, row, k)
-            values = kv[pl.ds(low_row, WINDOW), dv_heads]
-            dprobs = lax.dot_general(values, u, NT, preferred_element_type=jnp.float32)
-            probs_rounded = pt[k]
-            probs = probs_rounded.astype(jnp.float32)
-            delta = jnp.sum(probs * dprobs, axis=0, keepdims=True)
-            dscores = (probs * (dprobs - delta)).astype(jnp.bfloat16)
-            acc[pl.ds(low_row, WINDOW), heads] += jnp.dot(
-                dscores, stacked(q, row, k), preferred_element_type=jnp.float32
-            )
-            acc[pl.ds(low_row, WINDOW), dv_heads] += jnp.dot(
-                probs_rounded, u, preferred_element_type=jnp.float32
-            )
+                for k in group:
+                    hop(chunk, row, k).wait_recv()
+
+            for k in group:
+                heads = slice(k * HEAD_DIM, (k + 1) * HEAD_DIM)
+                dv_heads = slice(width + k * HEAD_DIM, width + (k + 1) * HEAD_DIM)
+                u = stacked(up, row, k)
+                values = kv[pl.ds(low_row, WINDOW), dv_heads]
+                dprobs = lax.dot_general(values, u, NT, preferred_element_type=jnp.float32)
+                probs_rounded = pt[k]
+                probs = probs_rounded.astype(jnp.float32)
+                delta = jnp.sum(probs * dprobs, axis=0, keepdims=True)
+                dscores = (probs * (dprobs - delta)).astype(jnp.bfloat16)
+                acc[pl.ds(low_row, WINDOW), heads] += jnp.dot(
+                    dscores, stacked(q, row, k), preferred_element_type=jnp.float32
+                )
+                acc[pl.ds(low_row, WINDOW), dv_heads] += jnp.dot(
+                    probs_rounded, u, preferred_element_type=jnp.float32
+                )
         dkeys = acc[pl.ds(row, ROWS), :width] * (1.0 / HEAD_DIM**0.5)
         dkv = jnp.concatenate([dkeys, acc[pl.ds(row, ROWS), width:]], axis=1).astype(jnp.bfloat16)
         for k in range(KV_HEADS):
@@ -254,8 +332,14 @@
         return carry
 
     lax.fori_loop(0, chunks, finish, 0)
-    for item in sent:
-        copy(*item).wait_send()
+    def all_sent(who):
+        for item in sent[who]:
+            copy(*item).wait_send()
+
+    all_sent("all")
+    pl.when(leading)(lambda: all_sent("leading"))
+    pl.when(jnp.logical_not(leading))(lambda: all_sent("following"))
+    pl.when(helping)(lambda: all_sent("helping"))
 
 
 def place_micros(order, grads, out, sem):
@@ -290,6 +374,7 @@
         out_specs=vmem,
         scratch_shapes=[
             pltpu.VMEM((fsdp, 2 * width, shard), bf16),
+            pltpu.VMEM((2 * width, shard), bf16),
             pltpu.VMEM((rows, features), bf16),
             pltpu.VMEM((rows, features), bf16),
             pltpu.VMEM((rows, features), bf16),
@@ -299,8 +384,8 @@
             pltpu.VMEM((KV_HEADS, WINDOW, GROUP * ROWS), bf16),
             pltpu.VMEM((rows, 2 * width), f32),
             pltpu.SemaphoreType.DMA((5,)),
-            pltpu.SemaphoreType.DMA((16, 3)),
-            pltpu.SemaphoreType.DMA((16, 3)),
+            pltpu.SemaphoreType.DMA((18, 3)),
+            pltpu.SemaphoreType.DMA((18, 3)),
             pltpu.SemaphoreType.DMA((chunks, KV_HEADS)),
             pltpu.SemaphoreType.DMA((chunks, KV_HEADS)),
         ],

time: 214 us -> 206 us (0.963)
  Pallas kernels: 214 us -> 206 us
    pallas_call x1, Pallas kernels: 211 us -> 203 us  [shards(): pl.pallas_call(functools.partial(kernel, sections, micros, tokens), out_s...]
where the time goes in v3:
time: 206 us
  Pallas kernels  206 us (100%)
    pallas_call x1, Pallas kernels, shards(): pl.pallas_call(functools.partial(kernel, sections, micros, tokens), out_s...  203 us

profile of v3, /device:TPU:0, one launch (start us, length us, event | category | flops | bytes accessed | tf_op | source)
XLA Modules:
  0.0 205.7 jit_solution(13515620448107727592)
XLA Ops:
  0.0 0.0 copy-start
  0.0 203.0 %chain.1.grads = bf16[256,8192]{1,0:T(8,128)(2,1)S(1)} custom-call(bf16[256,8192]{1,0:T(8,128)(2,1)} %bitcast.5, bf16[256,8192]{1,0:T(8,128)(2,1)} %bitcast.6, bf16[256,8192]{1,0:T(8,128)(2,1)} %bitcast.7, bf16[512,512]{1,0:T(8,128)(2,1)} %bitcast.8, bf16[512,512]{1,0:T(8,128)(2,1)} %bitcast.9, s32[2,1,4]{2,1,0:T(1,128)} %lens.1), custom_call_target="tpu_custom_call" | custom-call | tf_op jit(solution)/shard_map/chain/pallas_call | solution.py:370
  203.0 0.0 copy-done
  203.0 2.7 %order.2 = bf16[1,2,128,8192]{3,2,1,0:T(8,128)(2,1)} custom-call(s32[2]{0:T(128)S(1)} %copy-done, bf16[256,8192]{1,0:T(8,128)(2,1)S(1)} %chain.1.grads), custom_call_target="tpu_custom_call" | custom-call | tf_op jit(solution)/shard_map/order/pallas_call | solution.py:404
Async XLA Ops:
  0.0 203.0 %copy-start = (s32[2]{0:T(128)S(1)}, s32[2]{0:T(128)}, u32[]{:S(2)}) copy-start(s32[2]{0:T(128)} %order.3) | copy-start | bytes 28

commit v4 on v3

--- a/solution.py
+++ b/solution.py
@@ -22,7 +22,7 @@
 def kernel(
     sections, micros, tokens,
     acts_hbm, q_hbm, top_hbm, kw_hbm, vw_hbm, lens, down,
-    wt, relay, acts, q, up, raw, kv_acc, kv, pt, acc,
+    wt, relay, acts, q, up, raw, kv_acc, kv, pt, acc, total,
     load_sem, gather_send, gather_recv, chain_send, chain_recv,
 ):
     section, f = lax.axis_index("section"), lax.axis_index("fsdp")
@@ -271,42 +271,65 @@
 
     def step(chunk, carry):
         micro, first, row, low, low_row = place_of(chunk)
-        for group in ((0, 1, 2), (3,)):
-
-            @pl.when(section < sections - 1)
-            def _():
-                for k in group:
-                    hop(chunk, row, k).wait_recv()
-
-            for k in group:
+        def attend(k):
+            heads = slice(k * HEAD_DIM, (k + 1) * HEAD_DIM)
+            dv_heads = slice(width + k * HEAD_DIM, width + (k + 1) * HEAD_DIM)
+            u = stacked(up, row, k)
+            values = kv[pl.ds(low_row, WINDOW), dv_heads]
+            dprobs = lax.dot_general(values, u, NT, preferred_element_type=jnp.float32)
+            probs_rounded = pt[k]
+            probs = probs_rounded.astype(jnp.float32)
+            delta = jnp.sum(probs * dprobs, axis=0, keepdims=True)
+            dscores = (probs * (dprobs - delta)).astype(jnp.bfloat16)
+            acc[pl.ds(low_row, WINDOW), heads] += jnp.dot(
+                dscores, stacked(q, row, k), preferred_element_type=jnp.float32
+            )
+            acc[pl.ds(low_row, WINDOW), dv_heads] += jnp.dot(
+                probs_rounded, u, preferred_element_type=jnp.float32
+            )
+
+        @pl.when(section == sections - 1)
+        def _():
+            for k in range(KV_HEADS):
+                attend(k)
+            dkeys = acc[pl.ds(row, ROWS), :width] * (1.0 / HEAD_DIM**0.5)
+            dkv = jnp.concatenate([dkeys, acc[pl.ds(row, ROWS), width:]], axis=1).astype(jnp.bfloat16)
+            for k in range(KV_HEADS):
+                for owner in range(k * piece // shard, (k + 1) * piece // shard):
+                    cols = slice(owner * shard, (owner + 1) * shard)
+                    back = jnp.dot(dkv, wt[owner], preferred_element_type=jnp.float32)
+                    down[pl.ds(row, ROWS), cols] = (
+                        up[pl.ds(row, ROWS), cols].astype(jnp.float32) + back
+                    ).astype(jnp.bfloat16)
+                hop(chunk, row, k).start()
+
+        @pl.when(section < sections - 1)
+        def _():
+            for k in range(KV_HEADS):
+                hop(chunk, row, k).wait_recv()
+                attend(k)
                 heads = slice(k * HEAD_DIM, (k + 1) * HEAD_DIM)
                 dv_heads = slice(width + k * HEAD_DIM, width + (k + 1) * HEAD_DIM)
-                u = stacked(up, row, k)
-                values = kv[pl.ds(low_row, WINDOW), dv_heads]
-                dprobs = lax.dot_general(values, u, NT, preferred_element_type=jnp.float32)
-                probs_rounded = pt[k]
-                probs = probs_rounded.astype(jnp.float32)
-                delta = jnp.sum(probs * dprobs, axis=0, keepdims=True)
-                dscores = (probs * (dprobs - delta)).astype(jnp.bfloat16)
-                acc[pl.ds(low_row, WINDOW), heads] += jnp.dot(
-                    dscores, stacked(q, row, k), preferred_element_type=jnp.float32
-                )
-                acc[pl.ds(low_row, WINDOW), dv_heads] += jnp.dot(
-                    probs_rounded, u, preferred_element_type=jnp.float32
-                )
-        dkeys = acc[pl.ds(row, ROWS), :width] * (1.0 / HEAD_DIM**0.5)
-        dkv = jnp.concatenate([dkeys, acc[pl.ds(row, ROWS), width:]], axis=1).astype(jnp.bfloat16)
-        for k in range(KV_HEADS):
-            for owner in range(k * piece // shard, (k + 1) * piece // shard):
-                cols = slice(owner * shard, (owner + 1) * shard)
-                back = jnp.dot(dkv, wt[owner], preferred_element_type=jnp.float32)
-                down[pl.ds(row, ROWS), cols] = (
-                    up[pl.ds(row, ROWS), cols].astype(jnp.float32) + back
-                ).astype(jnp.bfloat16)
-
-            @pl.when(section > 0)
-            def _():
-                hop(chunk, row, k).start()
+                dkeys = acc[pl.ds(row, ROWS), heads] * (1.0 / HEAD_DIM**0.5)
+                dkv = jnp.concatenate([dkeys, acc[pl.ds(row, ROWS), dv_heads]], axis=1).astype(jnp.bfloat16)
+                for owner in range(wt.shape[0]):
+                    cols = slice(owner * shard, (owner + 1) * shard)
+                    weights = jnp.concatenate([wt[owner, heads, :], wt[owner, dv_heads, :]], axis=0)
+                    back = jnp.dot(dkv, weights, preferred_element_type=jnp.float32)
+                    if owner * shard // piece == k:
+                        back += up[pl.ds(row, ROWS), cols].astype(jnp.float32)
+                    if k > 0:
+                        back += total[:, cols]
+                    if k < KV_HEADS - 1:
+                        total[:, cols] = back
+                    else:
+                        down[pl.ds(row, ROWS), cols] = back.astype(jnp.bfloat16)
+                    done, rest = divmod((owner + 1) * shard, piece)
+                    if k == KV_HEADS - 1 and rest == 0:
+
+                        @pl.when(section > 0)
+                        def _():
+                            hop(chunk, row, done - 1).start()
 
         @pl.when(chunk < chunks - 1)
         def _():
@@ -383,6 +406,7 @@
             pltpu.VMEM((rows, 2 * width), bf16),
             pltpu.VMEM((KV_HEADS, WINDOW, GROUP * ROWS), bf16),
             pltpu.VMEM((rows, 2 * width), f32),
+            pltpu.VMEM((ROWS, features), f32),
             pltpu.SemaphoreType.DMA((5,)),
             pltpu.SemaphoreType.DMA((18, 3)),
             pltpu.SemaphoreType.DMA((18, 3)),

time: 206 us -> 202 us (0.981)
  Pallas kernels: 206 us -> 202 us
    pallas_call x1, Pallas kernels: 203 us -> 199 us  [shards(): pl.pallas_call(functools.partial(kernel, sections, micros, tokens), out_s...]
where the time goes in v4:
time: 202 us
  Pallas kernels  202 us (100%)
    pallas_call x1, Pallas kernels, shards(): pl.pallas_call(functools.partial(kernel, sections, micros, tokens), out_s...  199 us

profile of v4, /device:TPU:0, one launch (start us, length us, event | category | flops | bytes accessed | tf_op | source)
XLA Modules:
  0.0 201.6 jit_solution(10605518922571006673)
XLA Ops:
  0.0 0.0 copy-start
  0.0 198.9 %chain.1.grads = bf16[256,8192]{1,0:T(8,128)(2,1)S(1)} custom-call(bf16[256,8192]{1,0:T(8,128)(2,1)} %bitcast.5, bf16[256,8192]{1,0:T(8,128)(2,1)} %bitcast.6, bf16[256,8192]{1,0:T(8,128)(2,1)} %bitcast.7, bf16[512,512]{1,0:T(8,128)(2,1)} %bitcast.8, bf16[512,512]{1,0:T(8,128)(2,1)} %bitcast.9, s32[2,1,4]{2,1,0:T(1,128)} %lens.1), custom_call_target="tpu_custom_call" | custom-call | tf_op jit(solution)/shard_map/chain/pallas_call | solution.py:393
  198.9 0.0 copy-done
  198.9 2.7 %order.2 = bf16[1,2,128,8192]{3,2,1,0:T(8,128)(2,1)} custom-call(s32[2]{0:T(128)S(1)} %copy-done, bf16[256,8192]{1,0:T(8,128)(2,1)S(1)} %chain.1.grads), custom_call_target="tpu_custom_call" | custom-call | tf_op jit(solution)/shard_map/order/pallas_call | solution.py:428
Async XLA Ops:
  0.0 198.9 %copy-start = (s32[2]{0:T(128)S(1)}, s32[2]{0:T(128)}, u32[]{:S(2)}) copy-start(s32[2]{0:T(128)} %order.3) | copy-start | bytes 28

commit v5 on v4

--- a/solution.py
+++ b/solution.py
@@ -23,7 +23,7 @@
     sections, micros, tokens,
     acts_hbm, q_hbm, top_hbm, kw_hbm, vw_hbm, lens, down,
     wt, relay, acts, q, up, raw, kv_acc, kv, pt, acc, total,
-    load_sem, gather_send, gather_recv, chain_send, chain_recv,
+    load_sem, gather_send, gather_recv, chain_send, chain_recv, turn,
 ):
     section, f = lax.axis_index("section"), lax.axis_index("fsdp")
     z, h, c = f // 4, (f // 2) % 2, f % 2
@@ -76,8 +76,8 @@
         pl.semaphore_wait(barrier, 6)
 
     places = [(0, 0), (-1, 0), (1, 0), (0, 1), (2, 0), (1, 1), (-1, 1), (2, 1)]
-    third = (2 * width // 3) // 16 * 16
-    parts = [(0, third), (third, third), (2 * third, 2 * width - 2 * third)]
+    third = 3 * width // 4
+    parts = [(0, 2 * width - 2 * third), (2 * width - 2 * third, third), (2 * width - third, third)]
     from_0, from_1, from_2 = (0, 1, 2), (1, 2, 0), (2, 0, 1)
 
     def copy(role, part, owner, device):
@@ -115,6 +115,16 @@
             kv_acc[...] += lax.dot_general(
                 acts[:, cols], wt[owner], NT, preferred_element_type=jnp.float32
             )
+
+    def add_part(place, part, dc):
+        if dc == 1:
+            arrive(8 + place, part, place, core_pair, 1)
+        owner = (others if dc else owners)[place]
+        cols = pl.ds(pl.multiple_of(owner * shard, shard), shard)
+        rows = slice(parts[part][0], sum(parts[part]))
+        kv_acc[:, rows] += lax.dot_general(
+            acts[:, cols], wt[owner, rows, :], NT, preferred_element_type=jnp.float32
+        )
 
     for load in loads[2:]:
         load.start()
@@ -199,31 +209,25 @@
             to_core(6, from_0[i], "following")
             to_core(5, from_1[i], "following")
             to_core(4, from_2[i], "following")
-
-    @pl.when(leading)
-    def _():
-        for i in range(3):
-            arrive(3, from_1[i], 6, z_prev)
-            to_core(6, from_1[i], "leading")
-            arrive(5, from_1[i], 5, z_next)
-            to_core(5, from_1[i], "leading")
-
-    for place in (4, 6, 5):
-        add_keyval(place)
-
-    @pl.when(jnp.logical_not(leading))
-    def _():
+        for place in (4, 6, 5):
+            add_keyval(place)
         for part, device in zip(from_0, (z_prev, z_next, x_pair)):
             arrive(6, part, 7, device)
             to_core(7, part, "following")
+        add_keyval(7)
 
     @pl.when(leading)
     def _():
-        for part in from_0:
-            arrive(4, part, 7, x_pair)
-            to_core(7, part, "leading")
-
-    add_keyval(7)
+        add_keyval(4)
+        for i in range(3):
+            landed = ((6, from_1[i], 3, z_prev), (5, from_1[i], 5, z_next), (7, from_0[i], 4, x_pair))
+            for place, part, role, device in landed:
+                arrive(role, part, place, device)
+                to_core(place, part, "leading")
+            for dc in range(2):
+                for place, part, _, _ in landed:
+                    add_part(place, part, dc)
+
     kv[...] = kv_acc[...].astype(jnp.bfloat16)
 
     def place_of(chunk):
@@ -259,7 +263,7 @@
             s = jnp.where(allowed, s * (math.log2(math.e) / HEAD_DIM**0.5), -1e30)
             weights = jnp.exp2(s - jnp.max(s, axis=0, keepdims=True))
             probs = weights / jnp.sum(weights, axis=0, keepdims=True)
-            pt[k] = probs.astype(jnp.bfloat16)
+            pt[k] = probs
 
     def hop(chunk, row, k):
         block = pl.ds(row, ROWS), pl.ds(k * piece, piece)
@@ -277,8 +281,8 @@
             u = stacked(up, row, k)
             values = kv[pl.ds(low_row, WINDOW), dv_heads]
             dprobs = lax.dot_general(values, u, NT, preferred_element_type=jnp.float32)
-            probs_rounded = pt[k]
-            probs = probs_rounded.astype(jnp.float32)
+            probs = pt[k]
+            probs_rounded = probs.astype(jnp.bfloat16)
             delta = jnp.sum(probs * dprobs, axis=0, keepdims=True)
             dscores = (probs * (dprobs - delta)).astype(jnp.bfloat16)
             acc[pl.ds(low_row, WINDOW), heads] += jnp.dot(
@@ -292,6 +296,8 @@
         def _():
             for k in range(KV_HEADS):
                 attend(k)
+            pl.semaphore_signal(turn, inc=1, device_id=core_pair, device_id_type=MESH)
+            pl.semaphore_wait(turn, 1)
             dkeys = acc[pl.ds(row, ROWS), :width] * (1.0 / HEAD_DIM**0.5)
             dkv = jnp.concatenate([dkeys, acc[pl.ds(row, ROWS), width:]], axis=1).astype(jnp.bfloat16)
             for k in range(KV_HEADS):
@@ -306,8 +312,12 @@
         @pl.when(section < sections - 1)
         def _():
             for k in range(KV_HEADS):
+                if k == 0:
+                    pl.semaphore_signal(turn, inc=1, device_id=core_pair, device_id_type=MESH)
                 hop(chunk, row, k).wait_recv()
                 attend(k)
+                if k == 3:
+                    pl.semaphore_wait(turn, 1)
                 heads = slice(k * HEAD_DIM, (k + 1) * HEAD_DIM)
                 dv_heads = slice(width + k * HEAD_DIM, width + (k + 1) * HEAD_DIM)
                 dkeys = acc[pl.ds(row, ROWS), heads] * (1.0 / HEAD_DIM**0.5)
@@ -369,11 +379,12 @@
     _, micros, tokens, _ = out.shape
 
     def copies():
+        rows = tokens // sem.shape[1]
         for k in range(micros):
-            for i in range(tokens // ROWS):
-                row = pl.multiple_of(order[k] * tokens + i * ROWS, ROWS)
+            for i in range(sem.shape[1]):
+                row = pl.multiple_of(order[k] * tokens + i * rows, rows)
                 yield pltpu.make_async_copy(
-                    grads.at[pl.ds(row, ROWS)], out.at[0, k, pl.ds(i * ROWS, ROWS)], sem.at[k, i]
+                    grads.at[pl.ds(row, rows)], out.at[0, k, pl.ds(i * rows, rows)], sem.at[k, i]
                 )
 
     for copy in copies():
@@ -404,7 +415,7 @@
             pltpu.VMEM((2, shard, width), bf16),
             pltpu.VMEM((rows, 2 * width), f32),
             pltpu.VMEM((rows, 2 * width), bf16),
-            pltpu.VMEM((KV_HEADS, WINDOW, GROUP * ROWS), bf16),
+            pltpu.VMEM((KV_HEADS, WINDOW, GROUP * ROWS), f32),
             pltpu.VMEM((rows, 2 * width), f32),
             pltpu.VMEM((ROWS, features), f32),
             pltpu.SemaphoreType.DMA((5,)),
@@ -412,6 +423,7 @@
             pltpu.SemaphoreType.DMA((18, 3)),
             pltpu.SemaphoreType.DMA((chunks, KV_HEADS)),
             pltpu.SemaphoreType.DMA((chunks, KV_HEADS)),
+            pltpu.SemaphoreType.REGULAR,
         ],
         compiler_params=pltpu.CompilerParams(
             collective_id=0, has_side_effects=True, vmem_limit_bytes=56 << 20
@@ -430,7 +442,7 @@
         out_shape=jax.ShapeDtypeStruct((1, micros, tokens, features), bf16),
         in_specs=[pl.BlockSpec(memory_space=pltpu.SMEM), vmem],
         out_specs=hbm,
-        scratch_shapes=[pltpu.SemaphoreType.DMA((micros, tokens // ROWS))],
+        scratch_shapes=[pltpu.SemaphoreType.DMA((micros, 2))],
         compiler_params=pltpu.CompilerParams(vmem_limit_bytes=4 << 20),
         name="order",
     )(order, grads)

time: 202 us -> 202 us (level)
  no operation moved by 1% of the time
where the time goes in v5:
time: 202 us; the launch traced here: 201 us
  Pallas kernels  201 us (100%)
    pallas_call x1, Pallas kernels, shards(): pl.pallas_call(functools.partial(kernel, sections, micros, tokens), out_s...  199 us

profile of v5, /device:TPU:0, one launch (start us, length us, event | category | flops | bytes accessed | tf_op | source)
XLA Modules:
  0.0 201.4 jit_solution(6976658355706772078)
XLA Ops:
  0.0 0.0 copy-start
  0.0 198.6 %chain.1.grads = bf16[256,8192]{1,0:T(8,128)(2,1)S(1)} custom-call(bf16[256,8192]{1,0:T(8,128)(2,1)} %bitcast.5, bf16[256,8192]{1,0:T(8,128)(2,1)} %bitcast.6, bf16[256,8192]{1,0:T(8,128)(2,1)} %bitcast.7, bf16[512,512]{1,0:T(8,128)(2,1)} %bitcast.8, bf16[512,512]{1,0:T(8,128)(2,1)} %bitcast.9, s32[2,1,4]{2,1,0:T(1,128)} %lens.1), custom_call_target="tpu_custom_call" | custom-call | tf_op jit(solution)/shard_map/chain/pallas_call | solution.py:404
  198.7 0.0 copy-done
  198.7 2.6 %order.2 = bf16[1,2,128,8192]{3,2,1,0:T(8,128)(2,1)} custom-call(s32[2]{0:T(128)S(1)} %copy-done, bf16[256,8192]{1,0:T(8,128)(2,1)S(1)} %chain.1.grads), custom_call_target="tpu_custom_call" | custom-call | tf_op jit(solution)/shard_map/order/pallas_call | solution.py:440
Async XLA Ops:
  0.0 198.7 %copy-start = (s32[2]{0:T(128)S(1)}, s32[2]{0:T(128)}, u32[]{:S(2)}) copy-start(s32[2]{0:T(128)} %order.3) | copy-start | bytes 28

commit v6 on v5

--- a/solution.py
+++ b/solution.py
@@ -314,10 +314,10 @@
             for k in range(KV_HEADS):
                 if k == 0:
                     pl.semaphore_signal(turn, inc=1, device_id=core_pair, device_id_type=MESH)
+                if k == KV_HEADS - 1:
+                    pl.semaphore_wait(turn, 1)
                 hop(chunk, row, k).wait_recv()
                 attend(k)
-                if k == 3:
-                    pl.semaphore_wait(turn, 1)
                 heads = slice(k * HEAD_DIM, (k + 1) * HEAD_DIM)
                 dv_heads = slice(width + k * HEAD_DIM, width + (k + 1) * HEAD_DIM)
                 dkeys = acc[pl.ds(row, ROWS), heads] * (1.0 / HEAD_DIM**0.5)

time: 202 us -> 201 us (level)
  no operation moved by 1% of the time
where the time goes in v6:
time: 201 us
  Pallas kernels  201 us (100%)
    pallas_call x1, Pallas kernels, shards(): pl.pallas_call(functools.partial(kernel, sections, micros, tokens), out_s...  198 us

profile of v6, /device:TPU:0, one launch (start us, length us, event | category | flops | bytes accessed | tf_op | source)
XLA Modules:
  0.0 201.2 jit_solution(10249679270868142774)
XLA Ops:
  0.0 0.0 copy-start
  0.0 198.4 %chain.1.grads = bf16[256,8192]{1,0:T(8,128)(2,1)S(1)} custom-call(bf16[256,8192]{1,0:T(8,128)(2,1)} %bitcast.5, bf16[256,8192]{1,0:T(8,128)(2,1)} %bitcast.6, bf16[256,8192]{1,0:T(8,128)(2,1)} %bitcast.7, bf16[512,512]{1,0:T(8,128)(2,1)} %bitcast.8, bf16[512,512]{1,0:T(8,128)(2,1)} %bitcast.9, s32[2,1,4]{2,1,0:T(1,128)} %lens.1), custom_call_target="tpu_custom_call" | custom-call | tf_op jit(solution)/shard_map/chain/pallas_call | solution.py:404
  198.5 0.0 copy-done
  198.5 2.6 %order.2 = bf16[1,2,128,8192]{3,2,1,0:T(8,128)(2,1)} custom-call(s32[2]{0:T(128)S(1)} %copy-done, bf16[256,8192]{1,0:T(8,128)(2,1)S(1)} %chain.1.grads), custom_call_target="tpu_custom_call" | custom-call | tf_op jit(solution)/shard_map/order/pallas_call | solution.py:440
Async XLA Ops:
  0.0 198.5 %copy-start = (s32[2]{0:T(128)S(1)}, s32[2]{0:T(128)}, u32[]{:S(2)}) copy-start(s32[2]{0:T(128)} %order.3) | copy-start | bytes 28
